TPU v7x, 128 devices: a whole 4x4x4 slice. The times are simulated.
128 devices in a mesh: outer: 8 (over y_lo, x), inner: 16 (over z, y_hi, core).
Axes of the slice: x: 4, y: 4 (y_hi: 2, y_lo: 2; y = y_hi * 2 + y_lo), z: 4, core: 2. Of those that a mesh axis runs over, the one named last changes fastest.
Arguments:
- queries: bfloat16 [16384, 1536], P(('outer', 'inner')), may hold values from -6.2 to 6.2
- keys: bfloat16 [16384, 128], P(('outer', 'inner')), may hold values from -4 to 4
- values: bfloat16 [16384, 128], P(('outer', 'inner')), may hold values from -6 to 6
- doc_lengths: int32 [16], replicated, may hold values from 1 to 8192, 16384 in all
Outputs:
- attended: bfloat16 [16384, 1536], P(('outer', 'inner'))
Inputs may be any that keep to these rules, and one draw needn't show every extreme that they name: `doc_lengths`: 16 lengths summing to 16384; the longest is exactly 8192.
All inputs are finite; a program needn't handle non-finite values.
Results may differ from a plain program's by a relative error of at most 0.0059.
Values may be sent and summed in bfloat16 or wider, within the bound.
No kernel may reach another device: no remote copies, remote signals or barrier semaphores. Data moves between devices by JAX's collectives and lax.ppermute only.
A program may use at most 64 MiB of HBM per device.

v0:
```python
import functools
import math

import jax
import jax.numpy as jnp
from jax import lax
from jax.experimental import pallas as pl
from jax.experimental.pallas import tpu as pltpu
from jax.sharding import PartitionSpec as P

AXES = ("outer", "inner")
HEADS = 12
SIZE = 128
BLOCK = 128
SCALE = math.log2(math.e) / math.sqrt(SIZE)
MASKED = -1e30
EMPTY = -1e20
STEP = 4


def number(x, y, z, core):
    return ((y % 2) * 4 + x) * 16 + z * 4 + (y // 2) * 2 + core


def swap(array, partner):
    pairs = [
        (number(a, b, c, d), number(*partner(a, b, c, d)))
        for a in range(4)
        for b in range(4)
        for c in range(4)
        for d in range(2)
    ]
    return lax.ppermute(array, AXES, pairs)


def place(device):
    return device // 64, (device // 16) % 4, (device // 4) % 4, (device // 2) % 2, device % 2


def flag(condition):
    return jnp.where(condition, 1, 0).astype(jnp.int32)


def attend(stage, *refs):
    refs = list(refs)
    device_ref, docs_ref = refs[:2]
    refs = refs[2:]
    count = {"first": 4, "middle": 1, "last": 2}[stage]
    if stage == "first":
        own_ref, other_ref = refs[:2]
        pieces, refs = refs[2 : 2 + count], refs[2 + count :]
        rows, first_pos, query_pos, top, total, accum = refs[:6]
        refs = refs[6:]
    else:
        pieces, refs = refs[:count], refs[count:]
        rows, first_pos, query_pos, top_in, total_in, accum_in = refs[:6]
        refs = refs[6:]
        if stage == "last":
            own_out, own_stat, sent, top, total, accum = refs[:6]
            refs = refs[6:]
        else:
            top, total, accum = refs[:3]
            refs = refs[3:]
    window, bias, base_ref = refs
    device = device_ref[0]
    half, x, z, g, core = place(device)
    chip = device // 2

    lowest, highest = chip * 2 * BLOCK, chip * 2 * BLOCK + 2 * BLOCK - 1
    low_start, high_start, end = jnp.int32(0), jnp.int32(0), jnp.int32(0)
    ends = []
    for j in range(docs_ref.shape[0]):
        end = end + docs_ref[j]
        ends.append(end)
        low_start = jnp.where(lowest >= end, end, low_start)
        high_start = jnp.where(highest >= end, end, high_start)
    if stage == "first":
        token = lax.broadcasted_iota(jnp.int32, (2 * BLOCK, 128), 0)
        position = jnp.where(
            token < BLOCK, device * BLOCK + token, (chip * 4 + 1 - device) * BLOCK + token - BLOCK
        )
        start = jnp.zeros_like(position)
        for end in ends:
            start = jnp.where(position >= end, end, start)
        query_pos[...] = position
        first_pos[...] = start
        for h in range(HEADS):
            columns = slice(h * SIZE, (h + 1) * SIZE)
            rows[h * 256 : h * 256 + 128, :] = own_ref[:, columns]
            rows[h * 256 + 128 : h * 256 + 256, :] = other_ref[:, columns]
        top[...] = jnp.full_like(top, EMPTY)
        total[...] = jnp.zeros_like(total)
        accum[...] = jnp.zeros_like(accum)
    else:
        top[...] = top_in[...]
        total[...] = total_in[...]
        accum[...] = accum_in[...]

    def base(chosen, xs, zs, gs):
        return ((chosen * 4 + xs) * 16 + zs * 4 + gs * 2 + core) * BLOCK

    blocks = []
    if stage == "first":
        own = pieces[0]
        chosen = half * flag((g ^ 1) < g)
        blocks.append((own[half, 0], base(half, x, z, g)))
        blocks.append((own[chosen, 1], base(chosen, x, z, g ^ 1)))
        for k in (1, 2, 3):
            xs, zs = jnp.where(core == 0, x, x ^ k), jnp.where(core == 0, z ^ k, z)
            chosen = half * flag(xs * 4 + zs < x * 4 + z)
            for r in range(2):
                blocks.append((pieces[k][chosen, r], base(chosen, xs, zs, g ^ r)))
        blocks.append((own[1 - half, 0], base(1 - half, x, z, g)))
    else:
        for k, piece in zip((1,) if stage == "middle" else (3, 2), pieces, strict=True):
            for j in range(4):
                xs = jnp.where(core == 0, x ^ k, x ^ j)
                zs = jnp.where(core == 0, z ^ j, z ^ k)
                chosen = half * flag(xs * 4 + zs < x * 4 + z)
                for r in range(2):
                    blocks.append((piece[j, r], base(chosen, xs, zs, g ^ r)))
    for i, (values, begin) in enumerate(blocks):
        window[i * BLOCK : (i + 1) * BLOCK, :] = values
        base_ref[i] = begin

    def tile(offset, width, masked):
        key = window[pl.ds(offset, width), 0:128]
        value = window[pl.ds(offset, width), 128:256]
        scores = lax.dot_general(
            rows[...], key, (((1,), (1,)), ((), ())), preferred_element_type=jnp.float32
        )
        if masked:
            scores = scores + jnp.concatenate([bias[:, :width]] * HEADS, axis=0)
        before = top[...]
        fresh = jnp.maximum(before, jnp.max(scores, axis=1, keepdims=True) * SCALE)
        weights = jnp.exp2(scores * SCALE - jnp.concatenate([fresh] * (width // 128), axis=1))
        factor = jnp.exp2(before - fresh)
        part = weights[:, 0:128]
        for j in range(1, width // 128):
            part = part + weights[:, j * 128 : (j + 1) * 128]
        total[...] = total[...] * factor + part
        accum[...] = accum[...] * factor + lax.dot_general(
            weights.astype(jnp.bfloat16),
            value,
            (((1,), (0,)), ((), ())),
            preferred_element_type=jnp.float32,
        )
        top[...] = fresh

    def step(first, count):
        some, every = jnp.int32(0), jnp.int32(1)
        for j in range(count):
            begin = base_ref[first + j]
            some = some | flag((begin <= highest) & (begin + BLOCK - 1 >= low_start))
            every = every & flag((begin + BLOCK - 1 <= lowest) & (begin >= high_start))
        offset = first * BLOCK
        if not isinstance(first, int):
            offset = pl.multiple_of(offset, BLOCK)

        @pl.when((some == 1) & (every == 1))
        def _():
            tile(offset, count * BLOCK, False)

        @pl.when((some == 1) & (every == 0))
        def _():
            lane = lax.broadcasted_iota(jnp.int32, (2 * BLOCK, 128), 1)
            for j in range(count):
                key_pos = lane + base_ref[first + j]
                allowed = (key_pos >= first_pos[...]) & (key_pos <= query_pos[...])
                bias[:, j * 128 : (j + 1) * 128] = jnp.where(allowed, 0.0, MASKED)
            tile(offset, count * BLOCK, True)

    def advance(i, carry):
        step(i * STEP, STEP)
        return carry

    lax.fori_loop(0, len(blocks) // STEP, advance, 0)
    if len(blocks) % STEP:
        step(len(blocks) - 1, 1)

    if stage != "last":
        return
    lane = lax.broadcasted_iota(jnp.int32, (256, 128), 1)
    stat = jnp.zeros((256, 128), jnp.float32)
    for h in range(HEADS):
        columns = slice(h * SIZE, (h + 1) * SIZE)
        span = slice(h * 256, (h + 1) * 256)
        held = jnp.sum(total[span, :], axis=1, keepdims=True)
        filled = held > 0.0
        divisor = jnp.where(filled, held, 1.0)
        level = jnp.where(filled, top[span, :] + jnp.log2(divisor), EMPTY)
        stat = jnp.where(lane == h, level, stat)
        result = accum[span, :] / divisor
        own_out[:, columns] = result[:128, :]
        sent[:, columns] = result[128:, :].astype(jnp.bfloat16)
    own_stat[...] = stat[:128, :]
    rest = stat[128:, :]
    high = rest.astype(jnp.bfloat16)
    rest = rest - high.astype(jnp.float32)
    middle = rest.astype(jnp.bfloat16)
    low = (rest - middle.astype(jnp.float32)).astype(jnp.bfloat16)
    base_column = HEADS * SIZE
    sent[:, base_column : base_column + 128] = high
    sent[:, base_column + 128 : base_column + 256] = middle
    sent[:, base_column + 256 : base_column + 384] = low


def merge(own_ref, stat_ref, got_ref, out_ref):
    base_column = HEADS * SIZE
    other = (
        got_ref[:, base_column : base_column + 128].astype(jnp.float32)
        + got_ref[:, base_column + 128 : base_column + 256].astype(jnp.float32)
    ) + got_ref[:, base_column + 256 : base_column + 384].astype(jnp.float32)
    mine = stat_ref[...]
    peak = jnp.maximum(mine, other)
    left, right = jnp.exp2(mine - peak), jnp.exp2(other - peak)
    both = left + right
    left, right = left / both, right / both
    for h in range(HEADS):
        columns = slice(h * SIZE, (h + 1) * SIZE)
        out_ref[:, columns] = (
            own_ref[:, columns] * left[:, h : h + 1]
            + got_ref[:, columns].astype(jnp.float32) * right[:, h : h + 1]
        ).astype(jnp.bfloat16)


def call(stage, device, doc_lengths, arrays, state):
    smem = pl.BlockSpec(memory_space=pltpu.SMEM)
    vmem = pl.BlockSpec(memory_space=pltpu.VMEM)
    tokens = 2 * BLOCK
    rows = HEADS * tokens
    shape = jax.ShapeDtypeStruct
    sums = (shape((rows, SIZE), jnp.float32),) * 3
    blocks = {"first": 9, "middle": 8, "last": 16}[stage]
    aliases = {}
    if stage == "first":
        out_shape = (
            shape((rows, SIZE), jnp.bfloat16),
            shape((tokens, 128), jnp.int32),
            shape((tokens, 128), jnp.int32),
        ) + sums
    else:
        out_shape = sums
        if stage == "last":
            out_shape = (
                shape((BLOCK, HEADS * SIZE), jnp.float32),
                shape((BLOCK, 128), jnp.float32),
                shape((BLOCK, HEADS * SIZE + 384), jnp.bfloat16),
            ) + sums
        held = 2 + len(arrays) + 3
        aliases = {held + i: len(out_shape) - 3 + i for i in range(3)}
    keys = blocks * BLOCK
    return pl.pallas_call(
        functools.partial(attend, stage),
        out_shape=out_shape,
        in_specs=[smem, smem] + [vmem] * (len(arrays) + len(state)),
        out_specs=(vmem,) * len(out_shape),
        scratch_shapes=[
            pltpu.VMEM((keys, 2 * SIZE), jnp.bfloat16),
            pltpu.VMEM((tokens, STEP * BLOCK), jnp.float32),
            pltpu.SMEM((blocks,), jnp.int32),
        ],
        input_output_aliases=aliases,
        compiler_params=pltpu.CompilerParams(vmem_limit_bytes=40 * 2**20),
        cost_estimate=pl.CostEstimate(
            flops=4 * rows * keys * SIZE, bytes_accessed=4 * 2**20, transcendentals=rows * keys
        ),
    )(device, doc_lengths, *arrays, *state)


def body(queries, keys, values, doc_lengths):
    device = lax.axis_index(AXES).astype(jnp.int32)
    half, x, z, g, core = place(device)
    pair = jnp.pad(keys, ((0, 0), (0, SIZE))) + jnp.pad(values, ((0, 0), (SIZE, 0)))
    across = swap(pair, lambda x, y, z, c: (x, y ^ 1, z, c))
    other = swap(queries, lambda x, y, z, c: (x, y, z, 1 - c))
    both = jnp.stack([jnp.where(half == 0, pair, across), jnp.where(half == 0, across, pair)])
    far = swap(both, lambda x, y, z, c: (x, y ^ 3, z, c))
    plane = jnp.stack([both, far], axis=1)

    def along(array, k, second):
        return swap(
            array,
            lambda x, y, z, c: (x ^ k, y, z, c) if (c == 1) != second else (x, y, z ^ k, c),
        )

    order = (1, 3, 2)
    near = {k: along(plane, k, False) for k in order}
    line = [plane] + [near[k] for k in (1, 2, 3)]
    pieces = {}
    for k in order:
        chosen = []
        for j in range(4):
            xr, zr = jnp.where(core == 0, x ^ k, x), jnp.where(core == 0, z, z ^ k)
            xs, zs = jnp.where(core == 0, x, x ^ j), jnp.where(core == 0, z ^ j, z)
            second = (half == 1) & (xs * 4 + zs < xr * 4 + zr)
            chosen.append(jnp.where(second, line[j][1], line[j][0]))
        pieces[k] = along(jnp.stack(chosen), k, True)
    where = device.reshape(1)
    rows, first_pos, query_pos, *sums = call(
        "first", where, doc_lengths, [queries, other] + line, ()
    )
    fixed = [rows, first_pos, query_pos]
    sums = call("middle", where, doc_lengths, [pieces[1]], fixed + list(sums))
    own, stat, sent, *_ = call(
        "last", where, doc_lengths, [pieces[3], pieces[2]], fixed + list(sums)
    )
    got = swap(sent, lambda x, y, z, c: (x, y, z, 1 - c))
    vmem = pl.BlockSpec(memory_space=pltpu.VMEM)
    return pl.pallas_call(
        merge,
        out_shape=jax.ShapeDtypeStruct(queries.shape, jnp.bfloat16),
        in_specs=[vmem] * 3,
        out_specs=vmem,
    )(own, stat, got)


def solution(mesh):
    in_specs = (P(AXES, None), P(AXES, None), P(AXES, None), P())
    return jax.shard_map(
        body, mesh=mesh, in_specs=in_specs, out_specs=P(AXES, None), check_vma=False
    )
```

profile of v0, /device:TPU:95, one launch (start us, length us, event | category | flops | bytes accessed | tf_op | source)
XLA Modules:
  0.0 65.1 jit_solution(14816827863964471565)
XLA Ops:
  0.0 0.8 %pad_add_fusion = bf16[128,256]{1,0:T(8,128)(2,1)S(1)} fusion(bf16[128,128]{1,0:T(8,128)(2,1)} %param.6, bf16[128,128]{1,0:T(8,128)(2,1)} %param.5), kind=kLoop, calls=%fused_computation.25 | loop fusion | flops 131072 | bytes 131072 | tf_op jit(solution)/shard_map/add | solution.py:274
  0.8 0.5 collective-permute-start
  1.3 2.7 %collective-permute-done = bf16[128,256]{1,0:T(8,128)(2,1)S(1)} collective-permute-done((bf16[128,256]{1,0:T(8,128)(2,1)S(1)}, bf16[128,256]{1,0:T(8,128)(2,1)S(1)}, u32[]{:S(2)}, u32[]{:S(2)}) %collective-permute-start) | collective-permute-done | bytes 65568 | tf_op jit(solution)/shard_map/ppermute | solution.py:33
  4.0 0.8 %select_bitcast_fusion.1 = (bf16[1,128,256]{2,1,0:T(8,128)(2,1)S(1)}, bf16[1,128,256]{2,1,0:T(8,128)(2,1)S(1)}) fusion(bf16[128,256]{1,0:T(8,128)(2,1)S(1)} %collective-permute-done, pred[]{:T(512)S(6)} %eq.12, bf16[128,128]{1,0:T(8,128)(2,1)} %param.6, bf16[128,128]{1,0:T(8,128)(2,1)} %param.5), kind=kLoop, calls=%fused_computation.24 | loop fusion | flops 196608 | bytes 262145 | tf_op jit(solution)/shard_map/stack | solution.py:277
  4.8 0.1 collective-permute-start.1
  4.9 5.0 %collective-permute-done.1 = bf16[2,128,256]{2,1,0:T(8,128)(2,1)S(1)} collective-permute-done((bf16[2,128,256]{2,1,0:T(8,128)(2,1)S(1)}, bf16[2,128,256]{2,1,0:T(8,128)(2,1)S(1)}, u32[]{:S(2)}, u32[]{:S(2)}) %collective-permute-start.1) | collective-permute-done | bytes 131104 | tf_op jit(solution)/shard_map/ppermute | solution.py:33
  9.9 0.3 collective-permute-start.4
  10.2 2.9 %collective-permute-start.7 = (bf16[128,1536]{1,0:T(8,128)(2,1)}, bf16[128,1536]{1,0:T(8,128)(2,1)S(1)}, u32[]{:S(2)}, u32[]{:S(2)}) collective-permute-start(bf16[128,1536]{1,0:T(8,128)(2,1)} %refs_2_.1), channel_id=1, source_target_pairs={{0,1},{1,0},{4,5},{5,4},{8,9},{9,8},{12,13},{13,12},{64,65},{65,64... | collective-permute-start | bytes 1179656 | tf_op jit(solution)/shard_map/ppermute | solution.py:33
  13.1 1.1 %collective-permute-start.3 = (bf16[2,2,128,256]{3,2,1,0:T(8,128)(2,1)S(1)}, bf16[2,2,128,256]{3,2,1,0:T(8,128)(2,1)S(1)}, u32[]{:S(2)}, u32[]{:S(2)}) collective-permute-start(bf16[2,2,128,256]{3,2,1,0:T(8,128)(2,1)S(1)} %pad_maximum_fusion.3.refs_4_), channel_id=1, source_target_pairs={{0,8},{1,33},{4,12},{5,37},{8,0},{9,41},{12,4},{13,45},{64,72},{65... | collective-permute-start | bytes 786440 | tf_op jit(solution)/shard_map/ppermute | solution.py:33
  14.2 0.0 collective-permute-start.2
  14.3 2.2 %collective-permute-done.4.refs_7_ = bf16[2,2,128,256]{3,2,1,0:T(8,128)(2,1)S(1)} collective-permute-done((bf16[2,2,128,256]{3,2,1,0:T(8,128)(2,1)S(1)}, bf16[2,2,128,256]{3,2,1,0:T(8,128)(2,1)S(1)}, u32[]{:S(2)}, u32[]{:S(2)}) %collective-permute-start.4) | collective-permute-done | bytes 262176 | tf_op jit(solution)/shard_map/ppermute | solution.py:33
  16.5 4.2 %collective-permute-done.2.refs_5_ = bf16[2,2,128,256]{3,2,1,0:T(8,128)(2,1)S(1)} collective-permute-done((bf16[2,2,128,256]{3,2,1,0:T(8,128)(2,1)S(1)}, bf16[2,2,128,256]{3,2,1,0:T(8,128)(2,1)S(1)}, u32[]{:S(2)}, u32[]{:S(2)}) %collective-permute-start.2) | collective-permute-done | bytes 262176 | tf_op jit(solution)/shard_map/ppermute | solution.py:33
  20.8 0.0 collective-permute-done.3.refs_6_
  20.8 0.0 copy-start.2
  20.8 0.0 copy-start.3
  20.9 0.1 pad_maximum_fusion.2
  20.9 1.4 %collective-permute-start.8 = (bf16[4,2,128,256]{3,2,1,0:T(8,128)(2,1)S(1)}, bf16[4,2,128,256]{3,2,1,0:T(8,128)(2,1)S(1)}, u32[]{:S(2)}, u32[]{:S(2)}) collective-permute-start(bf16[4,2,128,256]{3,2,1,0:T(8,128)(2,1)S(1)} %pad_maximum_fusion.2), channel_id=1, source_target_pairs={{0,16},{1,5},{4,20},{5,1},{8,24},{9,13},{12,28},{13,9},{64,80},{65... | collective-permute-start | bytes 1572872 | tf_op jit(solution)/shard_map/ppermute | solution.py:33
  22.3 0.1 pad_maximum_fusion.1
  22.4 2.1 %collective-permute-start.6 = (bf16[4,2,128,256]{3,2,1,0:T(8,128)(2,1)S(1)}, bf16[4,2,128,256]{3,2,1,0:T(8,128)(2,1)S(1)}, u32[]{:S(2)}, u32[]{:S(2)}) collective-permute-start(bf16[4,2,128,256]{3,2,1,0:T(8,128)(2,1)S(1)} %pad_maximum_fusion.1), channel_id=1, source_target_pairs={{0,32},{1,9},{4,36},{5,13},{8,40},{9,1},{12,44},{13,5},{64,96},{65... | collective-permute-start | bytes 1572872 | tf_op jit(solution)/shard_map/ppermute | solution.py:33
  24.5 0.1 pad_maximum_fusion
  24.6 0.4 collective-permute-start.5
  24.9 0.0 collective-permute-done.7.refs_3_
  24.9 0.0 copy-done.2
  24.9 0.0 copy-done.3
  24.9 8.4 %shard_map.46 = (bf16[3072,128]{1,0:T(8,128)(2,1)S(1)}, s32[256,128]{1,0:T(8,128)S(1)}, s32[256,128]{1,0:T(8,128)S(1)}, f32[3072,128]{1,0:T(8,128)S(1)}, f32[307...) custom-call(s32[1]{0:T(128)} %bitcast.refs_0_, s32[16]{0:T(128)S(1)} %copy-done.2, bf16[128,1536]{1,0:T(8,128)(2,1)S(1)} %copy-done.3, ...), custom_call_target="tpu_custom_call" | custom-call | flops 1811939328 | bytes 4194304 | tf_op jit(solution)/shard_map/pallas_call | solution.py:253
  33.3 0.0 collective-permute-done.8.refs_2_
  33.3 7.1 %shard_map.47 = (f32[3072,128]{1,0:T(8,128)S(1)}, f32[3072,128]{1,0:T(8,128)S(1)}, f32[3072,128]{1,0:T(8,128)S(1)}) custom-call(s32[1]{0:T(128)} %bitcast.refs_0_, s32[16]{0:T(128)S(1)} %copy-done.2, bf16[4,2,128,256]{3,2,1,0:T(8,128)(2,1)S(1)} %collective-permute-done.8.refs_2_, ...), custom_call_target="tpu_custom_call", output_to_operand_aliasing={{0}: (6, {}), {1}: (7, {}), {2}: (8, {})} | custom-call | flops 1610612736 | bytes 4194304 | tf_op jit(solution)/shard_map/pallas_call | solution.py:253
  40.5 0.0 collective-permute-done.6.refs_3_
  40.5 0.0 collective-permute-done.5.refs_2_
  40.5 13.6 %shard_map.48 = (f32[128,1536]{1,0:T(8,128)S(1)}, f32[128,128]{1,0:T(8,128)S(1)}, bf16[128,1920]{1,0:T(8,128)(2,1)S(1)}, f32[3072,128]{1,0:T(8,128)S(1)}, f32[30...) custom-call(s32[1]{0:T(128)} %bitcast.refs_0_, ...), custom_call_target="tpu_custom_call", output_to_operand_aliasing={{3}: (7, {}), {4}: (8, {}), {5}: (9, {})} | custom-call | flops 3221225472 | bytes 4194304 | tf_op jit(solution)/shard_map/pallas_call | solution.py:253
  54.1 0.0 copy-start
  54.1 0.9 %copy-done = f32[128,1536]{1,0:T(8,128)} copy-done((f32[128,1536]{1,0:T(8,128)}, f32[128,1536]{1,0:T(8,128)S(1)}, u32[]{:S(2)}) %copy-start) | copy-done | bytes 786456
  55.0 0.0 copy-start.1
  55.0 0.6 copy-done.1
  55.6 4.7 %collective-permute-start.9 = (bf16[128,1920]{1,0:T(8,128)(2,1)S(1)}, bf16[128,1920]{1,0:T(8,128)(2,1)S(1)}, u32[]{:S(2)}, u32[]{:S(2)}) collective-permute-start(bf16[128,1920]{1,0:T(8,128)(2,1)S(1)} %get-tuple-element.28), channel_id=1, source_target_pairs={{0,1},{1,0},{4,5},{5,4},{8,9},{9,8},{12,13},{13,12},{64,65},{65,64... | collective-permute-start | bytes 1474568 | tf_op jit(solution)/shard_map/ppermute | solution.py:33
  60.3 1.5 %collective-permute-done.9.got_ref = bf16[128,1920]{1,0:T(8,128)(2,1)S(1)} collective-permute-done((bf16[128,1920]{1,0:T(8,128)(2,1)S(1)}, bf16[128,1920]{1,0:T(8,128)(2,1)S(1)}, u32[]{:S(2)}, u32[]{:S(2)}) %collective-permute-start.9) | collective-permute-done | bytes 491552 | tf_op jit(solution)/shard_map/ppermute | solution.py:33
  61.8 0.0 copy-start.4
  61.8 0.8 %copy-done.4 = bf16[128,1920]{1,0:T(8,128)(2,1)} copy-done((bf16[128,1920]{1,0:T(8,128)(2,1)}, bf16[128,1920]{1,0:T(8,128)(2,1)S(1)}, u32[]{:S(2)}) %copy-start.4) | copy-done | bytes 491544
  62.6 2.6 %shard_map.49 = bf16[128,1536]{1,0:T(8,128)(2,1)} custom-call(f32[128,1536]{1,0:T(8,128)} %copy-done, f32[128,128]{1,0:T(8,128)} %copy-done.1, bf16[128,1920]{1,0:T(8,128)(2,1)} %copy-done.4), custom_call_target="tpu_custom_call" | custom-call | tf_op jit(solution)/shard_map/pallas_call | solution.py:310
  (6 shorter events, 0.2 us)
Async XLA Ops:
  0.8 3.2 %collective-permute-start = (bf16[128,256]{1,0:T(8,128)(2,1)S(1)}, bf16[128,256]{1,0:T(8,128)(2,1)S(1)}, u32[]{:S(2)}, u32[]{:S(2)}) collective-permute-start(bf16[128,256]{1,0:T(8,128)(2,1)S(1)} %pad_add_fusion), channel_id=1, source_target_pairs={{0,64},{1,65},{4,68},{5,69},{8,72},{9,73},{12,76},{13,77},{64,0},{... | collective-permute-start | bytes 196616 | tf_op jit(solution)/shard_map/ppermute | solution.py:33
  4.8 5.1 %collective-permute-start.1 = (bf16[2,128,256]{2,1,0:T(8,128)(2,1)S(1)}, bf16[2,128,256]{2,1,0:T(8,128)(2,1)S(1)}, u32[]{:S(2)}, u32[]{:S(2)}) collective-permute-start(bf16[2,128,256]{2,1,0:T(8,128)(2,1)S(1)} %get-tuple-element.42), channel_id=1, source_target_pairs={{0,66},{1,67},{4,70},{5,71},{8,74},{9,75},{12,78},{13,79},{64,2},{... | collective-permute-start | bytes 393224 | tf_op jit(solution)/shard_map/ppermute | solution.py:33
  9.9 6.5 %collective-permute-start.4 = (bf16[2,2,128,256]{3,2,1,0:T(8,128)(2,1)S(1)}, bf16[2,2,128,256]{3,2,1,0:T(8,128)(2,1)S(1)}, u32[]{:S(2)}, u32[]{:S(2)}) collective-permute-start(bf16[2,2,128,256]{3,2,1,0:T(8,128)(2,1)S(1)} %pad_maximum_fusion.3.refs_4_), channel_id=1, source_target_pairs={{0,12},{1,49},{4,8},{5,53},{8,4},{9,57},{12,0},{13,61},{64,76},{65... | collective-permute-start | bytes 786440 | tf_op jit(solution)/shard_map/ppermute | solution.py:33
  10.2 14.7 %collective-permute-start.7 = (bf16[128,1536]{1,0:T(8,128)(2,1)}, bf16[128,1536]{1,0:T(8,128)(2,1)S(1)}, u32[]{:S(2)}, u32[]{:S(2)}) collective-permute-start(bf16[128,1536]{1,0:T(8,128)(2,1)} %refs_2_.1), channel_id=1, source_target_pairs={{0,1},{1,0},{4,5},{5,4},{8,9},{9,8},{12,13},{13,12},{64,65},{65,64... | collective-permute-start | bytes 1179656 | tf_op jit(solution)/shard_map/ppermute | solution.py:33
  13.1 7.7 %collective-permute-start.3 = (bf16[2,2,128,256]{3,2,1,0:T(8,128)(2,1)S(1)}, bf16[2,2,128,256]{3,2,1,0:T(8,128)(2,1)S(1)}, u32[]{:S(2)}, u32[]{:S(2)}) collective-permute-start(bf16[2,2,128,256]{3,2,1,0:T(8,128)(2,1)S(1)} %pad_maximum_fusion.3.refs_4_), channel_id=1, source_target_pairs={{0,8},{1,33},{4,12},{5,37},{8,0},{9,41},{12,4},{13,45},{64,72},{65... | collective-permute-start | bytes 786440 | tf_op jit(solution)/shard_map/ppermute | solution.py:33
  14.2 6.5 %collective-permute-start.2 = (bf16[2,2,128,256]{3,2,1,0:T(8,128)(2,1)S(1)}, bf16[2,2,128,256]{3,2,1,0:T(8,128)(2,1)S(1)}, u32[]{:S(2)}, u32[]{:S(2)}) collective-permute-start(bf16[2,2,128,256]{3,2,1,0:T(8,128)(2,1)S(1)} %pad_maximum_fusion.3.refs_4_), channel_id=1, source_target_pairs={{0,4},{1,17},{4,0},{5,21},{8,12},{9,25},{12,8},{13,29},{64,68},{65... | collective-permute-start | bytes 786440 | tf_op jit(solution)/shard_map/ppermute | solution.py:33
  20.8 4.1 %copy-start.2 = (s32[16]{0:T(128)S(1)}, s32[16]{0:T(128)}, u32[]{:S(2)}) copy-start(s32[16]{0:T(128)} %refs_1_.5) | copy-start | bytes 196
  20.8 4.1 %copy-start.3 = (bf16[128,1536]{1,0:T(8,128)(2,1)S(1)}, bf16[128,1536]{1,0:T(8,128)(2,1)}, u32[]{:S(2)}) copy-start(bf16[128,1536]{1,0:T(8,128)(2,1)} %refs_2_.1) | copy-start | bytes 1179652
  20.9 12.4 %collective-permute-start.8 = (bf16[4,2,128,256]{3,2,1,0:T(8,128)(2,1)S(1)}, bf16[4,2,128,256]{3,2,1,0:T(8,128)(2,1)S(1)}, u32[]{:S(2)}, u32[]{:S(2)}) collective-permute-start(bf16[4,2,128,256]{3,2,1,0:T(8,128)(2,1)S(1)} %pad_maximum_fusion.2), channel_id=1, source_target_pairs={{0,16},{1,5},{4,20},{5,1},{8,24},{9,13},{12,28},{13,9},{64,80},{65... | collective-permute-start | bytes 1572872 | tf_op jit(solution)/shard_map/ppermute | solution.py:33
  22.4 18.1 %collective-permute-start.6 = (bf16[4,2,128,256]{3,2,1,0:T(8,128)(2,1)S(1)}, bf16[4,2,128,256]{3,2,1,0:T(8,128)(2,1)S(1)}, u32[]{:S(2)}, u32[]{:S(2)}) collective-permute-start(bf16[4,2,128,256]{3,2,1,0:T(8,128)(2,1)S(1)} %pad_maximum_fusion.1), channel_id=1, source_target_pairs={{0,32},{1,9},{4,36},{5,13},{8,40},{9,1},{12,44},{13,5},{64,96},{65... | collective-permute-start | bytes 1572872 | tf_op jit(solution)/shard_map/ppermute | solution.py:33
  24.6 16.0 %collective-permute-start.5 = (bf16[4,2,128,256]{3,2,1,0:T(8,128)(2,1)S(1)}, bf16[4,2,128,256]{3,2,1,0:T(8,128)(2,1)S(1)}, u32[]{:S(2)}, u32[]{:S(2)}) collective-permute-start(bf16[4,2,128,256]{3,2,1,0:T(8,128)(2,1)S(1)} %pad_maximum_fusion), channel_id=1, source_target_pairs={{0,48},{1,13},{4,52},{5,9},{8,56},{9,5},{12,60},{13,1},{64,112},{6... | collective-permute-start | bytes 1572872 | tf_op jit(solution)/shard_map/ppermute | solution.py:33
  54.1 0.9 %copy-start = (f32[128,1536]{1,0:T(8,128)}, f32[128,1536]{1,0:T(8,128)S(1)}, u32[]{:S(2)}) copy-start(f32[128,1536]{1,0:T(8,128)S(1)} %get-tuple-element.26.own_ref) | copy-start | bytes 2359300
  55.0 0.6 copy-start.1
  55.6 6.2 %collective-permute-start.9 = (bf16[128,1920]{1,0:T(8,128)(2,1)S(1)}, bf16[128,1920]{1,0:T(8,128)(2,1)S(1)}, u32[]{:S(2)}, u32[]{:S(2)}) collective-permute-start(bf16[128,1920]{1,0:T(8,128)(2,1)S(1)} %get-tuple-element.28), channel_id=1, source_target_pairs={{0,1},{1,0},{4,5},{5,4},{8,9},{9,8},{12,13},{13,12},{64,65},{65,64... | collective-permute-start | bytes 1474568 | tf_op jit(solution)/shard_map/ppermute | solution.py:33
  61.8 0.8 %copy-start.4 = (bf16[128,1920]{1,0:T(8,128)(2,1)}, bf16[128,1920]{1,0:T(8,128)(2,1)S(1)}, u32[]{:S(2)}) copy-start(bf16[128,1920]{1,0:T(8,128)(2,1)S(1)} %collective-permute-done.9.got_ref) | copy-start | bytes 1474564
where the time goes:
time: 64.8 us; the launch traced here: 65.1 us
  Pallas kernels  31.7 us (49%)
  waiting for transfers between devices  15.6 us (24%)
  starting transfers between devices  13.4 us (21%)
  local copies, waits for them, and re-layouts  2.31 us (4%)
  other arithmetic  1.96 us (3%)
    pallas_call x3, Pallas kernels, call(): pl.pallas_call(functools.partial(attend, stage), out_shape=out_shape, in_...  29.1 us
    ppermute x10, waiting for transfers between devices, swap(): return lax.ppermute(array, AXES, pairs)  15.6 us
    ppermute x10, starting transfers between devices, swap(): return lax.ppermute(array, AXES, pairs)  13.4 us
    pallas_call x1, Pallas kernels, body(): pl.pallas_call(merge, out_shape=jax.ShapeDtypeStruct(queries.shape, jnp.b...  2.56 us
    unnamed x10, local copies, waits for them, and re-layouts  2.31 us
  transfers between devices with their start and end apart: 10, of which 5 were waited for; matrix products, arithmetic and copies ran while one was open for 1% of the time, Pallas kernels for 24%

commit v1 on v0

v1 whole, which is shorter than its diff:
```python
import functools
import math

import jax
import jax.numpy as jnp
from jax import lax
from jax.experimental import pallas as pl
from jax.experimental.pallas import tpu as pltpu
from jax.sharding import PartitionSpec as P

AXES = ("outer", "inner")
HEADS = 12
SIZE = 128
BLOCK = 128
SCALE = math.log2(math.e) / math.sqrt(SIZE)
MASKED = -1e30
EMPTY = -1e20
LEAST = 2.0**-80
MOST = 2.0**100
AFTER = 1 << 20
SIDES = 1
STEP = 4


def number(x, y, z, core):
    return ((y % 2) * 4 + x) * 16 + z * 4 + (y // 2) * 2 + core


def swap(array, partner):
    pairs = [
        (number(a, b, c, d), number(*partner(a, b, c, d)))
        for a in range(4)
        for b in range(4)
        for c in range(4)
        for d in range(2)
    ]
    return lax.ppermute(array, AXES, pairs)


def place(device):
    return device // 64, (device // 16) % 4, (device // 4) % 4, (device // 2) % 2, device % 2


def flag(condition):
    return jnp.where(condition, 1, 0).astype(jnp.int32)


def prepare(device_ref, docs_ref, queries_ref, unused_ref, rows, first_pos, query_pos):
    device = device_ref[0]
    chip = device // 2
    for h in range(HEADS):
        rows[h * BLOCK : (h + 1) * BLOCK, :] = queries_ref[:, h * SIZE : (h + 1) * SIZE]
    token = lax.broadcasted_iota(jnp.int32, (2 * BLOCK, 128), 0)
    position = jnp.where(
        token < BLOCK, device * BLOCK + token, (chip * 4 + 1 - device) * BLOCK + token - BLOCK
    )
    start = jnp.zeros_like(position)
    end = jnp.int32(0)
    for j in range(docs_ref.shape[0]):
        end = end + docs_ref[j]
        start = jnp.where(position >= end, end, start)
    query_pos[...] = position
    first_pos[...] = start


def blocks_of(stage, pieces, spot):
    half, x, z, g, core = spot

    def base(chosen, xs, zs, gs):
        return ((chosen * 4 + xs) * 16 + zs * 4 + gs * 2 + core) * BLOCK

    blocks = []
    if stage == "first":
        own = pieces[0]
        chosen = half * flag((g ^ 1) < g)
        blocks.append((own[half, 0], base(half, x, z, g)))
        blocks.append((own[chosen, 1], base(chosen, x, z, g ^ 1)))
        for k in (1, 2, 3):
            xs, zs = jnp.where(core == 0, x, x ^ k), jnp.where(core == 0, z ^ k, z)
            chosen = half * flag(xs * 4 + zs < x * 4 + z)
            for r in range(2):
                blocks.append((pieces[k][chosen, r], base(chosen, xs, zs, g ^ r)))
        blocks.append((own[1 - half, 0], base(1 - half, x, z, g)))
        return blocks
    for k, piece in zip((1,) if stage == "middle" else (3, 2), pieces, strict=True):
        for j in range(4):
            xs = jnp.where(core == 0, x ^ k, x ^ j)
            zs = jnp.where(core == 0, z ^ j, z ^ k)
            chosen = half * flag(xs * 4 + zs < x * 4 + z)
            for r in range(2):
                blocks.append((piece[j, r], base(chosen, xs, zs, g ^ r)))
    return blocks


def attend(stage, *refs):
    refs = list(refs)
    device_ref, docs_ref, first_pos, query_pos = refs[:4]
    refs = refs[4:]
    if stage == "first":
        own_ref, other_ref = refs[:2]
        pieces, refs = refs[2:6], refs[6:]
        rows, total, accum = refs[:3]
        window, bias, base_ref = refs[3:]
    else:
        rows, total_in, accum_in = refs[:3]
        refs = refs[3:]
        count = {"middle": 1, "last": 7}[stage]
        pieces, refs = refs[:count], refs[count:]
        if stage == "last":
            own_out, own_stat, sent = refs[:3]
            refs = refs[3:]
        total, accum = refs[:2]
        window, bias, base_ref = refs[2:5]
    device = device_ref[0]
    spot = place(device)
    chip = device // 2

    lowest, highest = chip * 2 * BLOCK, chip * 2 * BLOCK + 2 * BLOCK - 1
    low_start, high_start, end = jnp.int32(0), jnp.int32(0), jnp.int32(0)
    for j in range(docs_ref.shape[0]):
        end = end + docs_ref[j]
        low_start = jnp.where(lowest >= end, end, low_start)
        high_start = jnp.where(highest >= end, end, high_start)
    if stage == "first":
        rows[: HEADS * BLOCK, :] = own_ref[...]
        rows[HEADS * BLOCK :, :] = other_ref[...]

    def fill(blocks):
        for i, (values, begin) in enumerate(blocks):
            window[i * BLOCK : (i + 1) * BLOCK, :] = values
            base_ref[i] = begin

    def needed(first, count):
        some, every = jnp.int32(0), jnp.int32(1)
        for j in range(count):
            begin = base_ref[first + j]
            some = some | flag((begin <= highest) & (begin + BLOCK - 1 >= low_start))
            every = every & flag((begin + BLOCK - 1 <= lowest) & (begin >= high_start))
        return some, every

    def mask(first, count):
        lane = lax.broadcasted_iota(jnp.int32, (2 * BLOCK, 128), 1)
        for j in range(count):
            key_pos = lane + base_ref[first + j]
            allowed = (key_pos >= first_pos[...]) & (key_pos <= query_pos[...])
            bias[:, j * 128 : (j + 1) * 128] = jnp.where(allowed, 0.0, MASKED)

    def offset_of(first):
        return first * BLOCK if isinstance(first, int) else pl.multiple_of(first * BLOCK, BLOCK)

    def tile(first, count, masked, initial):
        width = count * BLOCK
        key = window[pl.ds(offset_of(first), width), 0:128]
        value = window[pl.ds(offset_of(first), width), 128:256]
        for side in range(SIDES):
            size = 2 * HEADS * BLOCK // SIDES
            span = slice(side * size, (side + 1) * size)
            scores = lax.dot_general(
                rows[span, :], key, (((1,), (1,)), ((), ())), preferred_element_type=jnp.float32
            )
            scores = scores * SCALE
            if masked:
                left, right = bias[:BLOCK, :width], bias[BLOCK:, :width]
                spread = ([left] * HEADS + [right] * HEADS)[
                    span.start // BLOCK : span.stop // BLOCK
                ]
                scores = scores + jnp.concatenate(spread, axis=0)
            weights = jnp.exp2(scores)
            part = weights[:, 0:128]
            for j in range(1, count):
                part = part + weights[:, j * 128 : (j + 1) * 128]
            product = jnp.dot(
                weights.astype(jnp.bfloat16), value, preferred_element_type=jnp.float32
            )
            if not initial:
                total[span, :] = total[span, :] + part
                accum[span, :] = accum[span, :] + product
            elif stage == "first":
                total[span, :] = part
                accum[span, :] = product
            else:
                total[span, :] = total_in[span, :] + part
                accum[span, :] = accum_in[span, :] + product

    def step(first, count, initial):
        some, every = needed(first, count)

        @pl.when((some == 1) & (every == 1))
        def _():
            tile(first, count, False, initial)

        @pl.when((some == 1) & (every == 0))
        def _():
            mask(first, count)
            tile(first, count, True, initial)

        if initial:

            @pl.when(some == 0)
            def _():
                if stage == "first":
                    total[...] = jnp.zeros_like(total)
                    accum[...] = jnp.zeros_like(accum)
                else:
                    total[...] = total_in[...]
                    accum[...] = accum_in[...]

    def advance(i, carry):
        step(i * STEP, STEP, False)
        return carry

    blocks = blocks_of(stage, pieces[:2] if stage == "last" else pieces, spot)
    fill(blocks)
    step(0, STEP, True)
    lax.fori_loop(1, len(blocks) // STEP, advance, 0)
    if len(blocks) % STEP:
        step(len(blocks) - 1, 1, False)
    if stage != "last":
        return

    top = refs[5]

    def finish(shifted):
        lane = lax.broadcasted_iota(jnp.int32, (BLOCK, 128), 1)
        bad = jnp.zeros((BLOCK, 1), jnp.int32)
        stats = []
        for side in range(2):
            stat = jnp.zeros((BLOCK, 128), jnp.float32)
            for h in range(HEADS):
                columns = slice(h * SIZE, (h + 1) * SIZE)
                span = slice((side * HEADS + h) * BLOCK, (side * HEADS + h + 1) * BLOCK)
                held = jnp.sum(total[span, :], axis=1, keepdims=True)
                fine = (held >= LEAST) & (held <= MOST)
                if side == 1:
                    fine = fine | (first_pos[BLOCK:, 0:1] >= (chip * 4 + 1 - device) * BLOCK)
                bad = jnp.where(fine, bad, 1)
                filled = held > 0.0
                divisor = jnp.where(filled, held, 1.0)
                level = jnp.log2(divisor)
                if shifted:
                    level = level + top[span, :]
                stat = jnp.where(lane == h, jnp.where(filled, level, EMPTY), stat)
                result = accum[span, :] * (1.0 / divisor)
                if side == 0:
                    own_out[:, columns] = result
                else:
                    sent[:, columns] = result.astype(jnp.bfloat16)
            stats.append(stat)
        own_stat[...] = stats[0]
        rest = stats[1]
        high = rest.astype(jnp.bfloat16)
        rest = rest - high.astype(jnp.float32)
        middle = rest.astype(jnp.bfloat16)
        low = (rest - middle.astype(jnp.float32)).astype(jnp.bfloat16)
        base_column = HEADS * SIZE
        sent[:, base_column : base_column + 128] = high
        sent[:, base_column + 128 : base_column + 256] = middle
        sent[:, base_column + 256 : base_column + 384] = low
        return jnp.max(bad)

    bad = finish(False)

    @pl.when(bad > 0)
    def _():
        top[...] = jnp.full_like(top, EMPTY)
        total[...] = jnp.zeros_like(total)
        accum[...] = jnp.zeros_like(accum)
        width = STEP * BLOCK

        def careful(i, carry):
            first = i * STEP
            mask(first, STEP)
            key = window[pl.ds(offset_of(first), width), 0:128]
            value = window[pl.ds(offset_of(first), width), 128:256]

            def head(t, carry):
                span = pl.ds(pl.multiple_of(t * BLOCK, BLOCK), BLOCK)
                side = pl.ds(pl.multiple_of(t // HEADS * BLOCK, BLOCK), BLOCK)
                scores = lax.dot_general(
                    rows[span, :],
                    key,
                    (((1,), (1,)), ((), ())),
                    preferred_element_type=jnp.float32,
                )
                scores = scores * SCALE + bias[side, :width]
                before = top[span, :]
                fresh = jnp.maximum(before, jnp.max(scores, axis=1, keepdims=True))
                weights = jnp.exp2(scores - jnp.concatenate([fresh] * STEP, axis=1))
                part = weights[:, 0:128]
                for j in range(1, STEP):
                    part = part + weights[:, j * 128 : (j + 1) * 128]
                factor = jnp.exp2(before - fresh)
                total[span, :] = total[span, :] * factor + part
                accum[span, :] = accum[span, :] * factor + jnp.dot(
                    weights.astype(jnp.bfloat16), value, preferred_element_type=jnp.float32
                )
                top[span, :] = fresh
                return carry

            lax.fori_loop(0, 2 * HEADS, head, 0)
            return carry

        for name, group in (("first", pieces[3:7]), ("middle", pieces[2:3]), ("last", pieces[:2])):
            again = blocks_of(name, group, spot)
            while len(again) % STEP:
                again.append((again[0][0], jnp.int32(AFTER)))
            fill(again)
            lax.fori_loop(0, len(again) // STEP, careful, 0)
        finish(True)


def merge(own_ref, stat_ref, got_ref, out_ref):
    base_column = HEADS * SIZE
    other = (
        got_ref[:, base_column : base_column + 128].astype(jnp.float32)
        + got_ref[:, base_column + 128 : base_column + 256].astype(jnp.float32)
    ) + got_ref[:, base_column + 256 : base_column + 384].astype(jnp.float32)
    mine = stat_ref[...]
    peak = jnp.maximum(mine, other)
    left, right = jnp.exp2(mine - peak), jnp.exp2(other - peak)
    both = left + right
    left, right = left / both, right / both
    for h in range(HEADS):
        columns = slice(h * SIZE, (h + 1) * SIZE)
        out_ref[:, columns] = (
            own_ref[:, columns] * left[:, h : h + 1]
            + got_ref[:, columns].astype(jnp.float32) * right[:, h : h + 1]
        ).astype(jnp.bfloat16)


def call(stage, scalars, arrays, pieces):
    smem = pl.BlockSpec(memory_space=pltpu.SMEM)
    vmem = pl.BlockSpec(memory_space=pltpu.VMEM)
    tokens = 2 * BLOCK
    rows = HEADS * tokens
    shape = jax.ShapeDtypeStruct
    out_shape = (shape((rows, SIZE), jnp.float32),) * 2
    blocks = {"first": 9, "middle": 8, "last": 16}[stage]
    scratch_shapes = [
        pltpu.VMEM((blocks * BLOCK, 2 * SIZE), jnp.bfloat16),
        pltpu.VMEM((tokens, STEP * BLOCK), jnp.float32),
        pltpu.SMEM((blocks,), jnp.int32),
    ]
    aliases = {}
    if stage == "first":
        out_shape = (shape((rows, SIZE), jnp.bfloat16),) + out_shape
    elif stage == "middle":
        aliases = {5: 0, 6: 1}
    else:
        out_shape = (
            shape((BLOCK, HEADS * SIZE), jnp.float32),
            shape((BLOCK, 128), jnp.float32),
            shape((BLOCK, HEADS * SIZE + 384), jnp.bfloat16),
        ) + out_shape
        aliases = {5: 3, 6: 4}
        scratch_shapes.append(pltpu.VMEM((rows, 128), jnp.float32))
    work = rows * blocks * BLOCK
    return pl.pallas_call(
        functools.partial(attend, stage),
        out_shape=out_shape,
        in_specs=[smem, smem] + [vmem] * (2 + len(arrays) + len(pieces)),
        out_specs=(vmem,) * len(out_shape),
        scratch_shapes=scratch_shapes,
        input_output_aliases=aliases,
        compiler_params=pltpu.CompilerParams(vmem_limit_bytes=40 * 2**20),
        cost_estimate=pl.CostEstimate(
            flops=4 * work * SIZE, bytes_accessed=4 * 2**20, transcendentals=work
        ),
    )(*scalars, *arrays, *pieces)


def body(queries, keys, values, doc_lengths):
    device = lax.axis_index(AXES).astype(jnp.int32)
    half, x, z, g, core = place(device)
    pair = jnp.pad(keys, ((0, 0), (0, SIZE))) + jnp.pad(values, ((0, 0), (SIZE, 0)))
    across = swap(pair, lambda x, y, z, c: (x, y ^ 1, z, c))
    both = jnp.stack([jnp.where(half == 0, pair, across), jnp.where(half == 0, across, pair)])
    far = swap(both, lambda x, y, z, c: (x, y ^ 3, z, c))
    plane = jnp.stack([both, far], axis=1)

    def along(array, k, second):
        return swap(
            array,
            lambda x, y, z, c: (x ^ k, y, z, c) if (c == 1) != second else (x, y, z ^ k, c),
        )

    order = (1, 3, 2)
    near = {k: along(plane, k, False) for k in order}
    line = [plane] + [near[k] for k in (1, 2, 3)]
    where = device.reshape(1)
    smem = pl.BlockSpec(memory_space=pltpu.SMEM)
    vmem = pl.BlockSpec(memory_space=pltpu.VMEM)
    positions = jax.ShapeDtypeStruct((2 * BLOCK, 128), jnp.int32)
    rows, first_pos, query_pos = pl.pallas_call(
        prepare,
        out_shape=(
            jax.ShapeDtypeStruct((HEADS * BLOCK, SIZE), jnp.bfloat16),
            positions,
            positions,
        ),
        in_specs=[smem, smem, vmem, pl.BlockSpec(memory_space=pl.ANY)],
        out_specs=(vmem,) * 3,
        compiler_params=pltpu.CompilerParams(vmem_limit_bytes=16 * 2**20),
    )(where, doc_lengths, queries, near[order[0]])
    other = swap(rows, lambda x, y, z, c: (x, y, z, 1 - c))
    pieces = {}
    for k in order:
        chosen = []
        for j in range(4):
            xr, zr = jnp.where(core == 0, x ^ k, x), jnp.where(core == 0, z, z ^ k)
            xs, zs = jnp.where(core == 0, x, x ^ j), jnp.where(core == 0, z ^ j, z)
            second = (half == 1) & (xs * 4 + zs < xr * 4 + zr)
            chosen.append(jnp.where(second, line[j][1], line[j][0]))
        pieces[k] = along(jnp.stack(chosen), k, True)
    scalars = [where, doc_lengths, first_pos, query_pos]
    rows, *sums = call("first", scalars, [rows, other], line)
    sums = call("middle", scalars, [rows, *sums], [pieces[1]])
    own, stat, sent, *_ = call(
        "last", scalars, [rows, *sums], [pieces[3], pieces[2], pieces[1], *line]
    )
    got = swap(sent, lambda x, y, z, c: (x, y, z, 1 - c))
    return pl.pallas_call(
        merge,
        out_shape=jax.ShapeDtypeStruct(queries.shape, jnp.bfloat16),
        in_specs=[vmem] * 3,
        out_specs=vmem,
        compiler_params=pltpu.CompilerParams(vmem_limit_bytes=16 * 2**20),
    )(own, stat, got)


def solution(mesh):
    in_specs = (P(AXES, None), P(AXES, None), P(AXES, None), P())
    return jax.shard_map(
        body, mesh=mesh, in_specs=in_specs, out_specs=P(AXES, None), check_vma=False
    )
```

time: 64.8 us -> 150 us (2.31)
  the two profiles are of different devices: /device:TPU:95 before, /device:TPU:57 now
where the time goes in v1:
time: 150 us; the launch traced here: 149 us
  Pallas kernels  113 us (75%)
  starting transfers between devices  17.3 us (12%)
  waiting for transfers between devices  17 us (11%)
  other arithmetic  1.96 us (1%)
    pallas_call x3, Pallas kernels, call(): pl.pallas_call(functools.partial(attend, stage), out_shape=out_shape, in_...  111 us
    ppermute x10, starting transfers between devices, swap(): return lax.ppermute(array, AXES, pairs)  17.3 us
    ppermute x10, waiting for transfers between devices, swap(): return lax.ppermute(array, AXES, pairs)  17 us
  transfers between devices with their start and end apart: 10, of which 7 were waited for; matrix products, arithmetic and copies ran while one was open for 0% of the time, Pallas kernels for 7%

profile of v1, /device:TPU:57, one launch (start us, length us, event | category | flops | bytes accessed | tf_op | source)
XLA Modules:
  0.0 149.4 jit_solution(13108248719371360709)
XLA Ops:
  0.0 0.8 pad_add_fusion
  0.8 0.5 collective-permute-start
  1.3 2.7 %collective-permute-done = bf16[128,256]{1,0:T(8,128)(2,1)S(1)} collective-permute-done((bf16[128,256]{1,0:T(8,128)(2,1)S(1)}, bf16[128,256]{1,0:T(8,128)(2,1)S(1)}, u32[]{:S(2)}, u32[]{:S(2)}) %collective-permute-start) | collective-permute-done | bytes 65568 | tf_op jit(solution)/shard_map/ppermute | solution.py:37
  4.0 0.8 select_bitcast_fusion.1
  4.8 0.1 collective-permute-start.1
  4.9 5.0 %collective-permute-done.1 = bf16[2,128,256]{2,1,0:T(8,128)(2,1)S(1)} collective-permute-done((bf16[2,128,256]{2,1,0:T(8,128)(2,1)S(1)}, bf16[2,128,256]{2,1,0:T(8,128)(2,1)S(1)}, u32[]{:S(2)}, u32[]{:S(2)}) %collective-permute-start.1) | collective-permute-done | bytes 131104 | tf_op jit(solution)/shard_map/ppermute | solution.py:37
  9.9 1.3 collective-permute-start.2
  11.2 1.8 %collective-permute-start.5 = (bf16[2,2,128,256]{3,2,1,0:T(8,128)(2,1)S(1)}, bf16[2,2,128,256]{3,2,1,0:T(8,128)(2,1)S(1)}, u32[]{:S(2)}, u32[]{:S(2)}) collective-permute-start(bf16[2,2,128,256]{3,2,1,0:T(8,128)(2,1)S(1)} %pad_maximum_fusion.3.refs_6_.refs_10_), channel_id=1, source_target_pairs={{0,12},{1,49},{4,8},{5,53},{8,4},{9,57},{12,0},{13,61},{64,76},{65... | collective-permute-start | bytes 786440 | tf_op jit(solution)/shard_map/ppermute | solution.py:37
  13.1 0.6 collective-permute-start.4
  13.7 0.0 copy-start
  13.7 0.0 copy-start.1
  13.7 1.5 %collective-permute-done.2.unused_ref.refs_7_.refs_11_ = bf16[2,2,128,256]{3,2,1,0:T(8,128)(2,1)S(1)} collective-permute-done((bf16[2,2,128,256]{3,2,1,0:T(8,128)(2,1)S(1)}, bf16[2,2,128,256]{3,2,1,0:T(8,128)(2,1)S(1)}, u32[]{:S(2)}, u32[]{:S(2)}) %collective-permute-start.2) | collective-permute-done | bytes 262176 | tf_op jit(solution)/shard_map/ppermute | solution.py:37
  15.3 5.1 %collective-permute-done.4.refs_8_.refs_12_ = bf16[2,2,128,256]{3,2,1,0:T(8,128)(2,1)S(1)} collective-permute-done((bf16[2,2,128,256]{3,2,1,0:T(8,128)(2,1)S(1)}, bf16[2,2,128,256]{3,2,1,0:T(8,128)(2,1)S(1)}, u32[]{:S(2)}, u32[]{:S(2)}) %collective-permute-start.4) | collective-permute-done | bytes 262176 | tf_op jit(solution)/shard_map/ppermute | solution.py:37
  20.4 0.1 collective-permute-done.5.refs_9_.refs_13_
  20.5 0.1 pad_maximum_fusion
  20.6 0.2 collective-permute-start.6
  20.8 0.0 copy-done
  20.8 0.0 copy-done.1
  20.8 0.8 shard_map.46
  21.6 5.9 %collective-permute-start.3 = (bf16[1536,128]{1,0:T(8,128)(2,1)S(1)}, bf16[1536,128]{1,0:T(8,128)(2,1)S(1)}, u32[]{:S(2)}, u32[]{:S(2)}) collective-permute-start(bf16[1536,128]{1,0:T(8,128)(2,1)S(1)} %get-tuple-element.18.refs_4_), channel_id=1, source_target_pairs={{0,1},{1,0},{4,5},{5,4},{8,9},{9,8},{12,13},{13,12},{64,65},{65,64... | collective-permute-start | bytes 1179656 | tf_op jit(solution)/shard_map/ppermute | solution.py:37
  27.5 0.1 pad_maximum_fusion.1
  27.6 0.6 collective-permute-start.7
  28.1 0.1 pad_maximum_fusion.2
  28.2 2.0 %collective-permute-start.8 = (bf16[4,2,128,256]{3,2,1,0:T(8,128)(2,1)S(1)}, bf16[4,2,128,256]{3,2,1,0:T(8,128)(2,1)S(1)}, u32[]{:S(2)}, u32[]{:S(2)}) collective-permute-start(bf16[4,2,128,256]{3,2,1,0:T(8,128)(2,1)S(1)} %pad_maximum_fusion.2), channel_id=1, source_target_pairs={{0,32},{1,9},{4,36},{5,13},{8,40},{9,1},{12,44},{13,5},{64,96},{65... | collective-permute-start | bytes 1572872 | tf_op jit(solution)/shard_map/ppermute | solution.py:37
  30.2 0.0 collective-permute-done.3.refs_5_
  30.2 4.9 %shard_map.47 = (bf16[3072,128]{1,0:T(8,128)(2,1)S(1)}, f32[3072,128]{1,0:T(8,128)S(1)}, f32[3072,128]{1,0:T(8,128)S(1)}) custom-call(s32[1]{0:T(128)} %bitcast.device_ref.refs_0_, s32[16]{0:T(128)S(1)} %copy-done.1, s32[256,128]{1,0:T(8,128)S(1)} %get-tuple-element.16.refs_2_, s32[256,128]{1,0:T(8,128)S(1)} %get-tuple-element.17.refs_3_, ...), custom_call_target="tpu_custom_call" | custom-call | flops 1811939328 | bytes 4194304 | tf_op jit(solution)/shard_map/pallas_call | solution.py:358
  35.1 0.0 collective-permute-done.6.refs_7_.refs_9_
  35.1 5.3 %shard_map.48 = (f32[3072,128]{1,0:T(8,128)S(1)}, f32[3072,128]{1,0:T(8,128)S(1)}) custom-call(s32[1]{0:T(128)} %bitcast.device_ref.refs_0_, s32[16]{0:T(128)S(1)} %copy-done.1, s32[256,128]{1,0:T(8,128)S(1)} %get-tuple-element.16.refs_2_, s32[256,128]{1,0:T(8,128)S(1)} %get-tuple-element.17.refs_3_, ...), custom_call_target="tpu_custom_call", output_to_operand_aliasing={{0}: (5, {}), {1}: (6, {})} | custom-call | flops 1610612736 | bytes 4194304 | tf_op jit(solution)/shard_map/pallas_call | solution.py:358
  40.4 1.2 collective-permute-done.7.refs_7_
  41.6 0.0 collective-permute-done.8.refs_8_
  41.6 100.7 %shard_map.49 = (f32[128,1536]{1,0:T(8,128)S(1)}, f32[128,128]{1,0:T(8,128)S(1)}, bf16[128,1920]{1,0:T(8,128)(2,1)S(1)}, f32[3072,128]{1,0:T(8,128)S(1)}, f32[3072,128]{1,0:T(8,128)S(1)}) custom-call(s32[1]{0:T(128)} %bitcast.device_ref.refs_0_, s32[16]{0:T(128)S(1)} %copy-done.1, ...), custom_call_target="tpu_custom_call", output_to_operand_aliasing={{3}: (5, {}), {4}: (6, {})} | custom-call | flops 3221225472 | bytes 4194304 | tf_op jit(solution)/shard_map/pallas_call | solution.py:358
  142.3 4.3 %collective-permute-start.9 = (bf16[128,1920]{1,0:T(8,128)(2,1)S(1)}, bf16[128,1920]{1,0:T(8,128)(2,1)S(1)}, u32[]{:S(2)}, u32[]{:S(2)}) collective-permute-start(bf16[128,1920]{1,0:T(8,128)(2,1)S(1)} %get-tuple-element.26), channel_id=1, source_target_pairs={{0,1},{1,0},{4,5},{5,4},{8,9},{9,8},{12,13},{13,12},{64,65},{65,64... | collective-permute-start | bytes 1474568 | tf_op jit(solution)/shard_map/ppermute | solution.py:37
  146.6 1.5 collective-permute-done.9.got_ref
  148.1 1.3 shard_map.50
  (6 shorter events, 0.2 us)
Async XLA Ops:
  0.8 3.2 %collective-permute-start = (bf16[128,256]{1,0:T(8,128)(2,1)S(1)}, bf16[128,256]{1,0:T(8,128)(2,1)S(1)}, u32[]{:S(2)}, u32[]{:S(2)}) collective-permute-start(bf16[128,256]{1,0:T(8,128)(2,1)S(1)} %pad_add_fusion), channel_id=1, source_target_pairs={{0,64},{1,65},{4,68},{5,69},{8,72},{9,73},{12,76},{13,77},{64,0},{... | collective-permute-start | bytes 196616 | tf_op jit(solution)/shard_map/ppermute | solution.py:37
  4.8 5.1 %collective-permute-start.1 = (bf16[2,128,256]{2,1,0:T(8,128)(2,1)S(1)}, bf16[2,128,256]{2,1,0:T(8,128)(2,1)S(1)}, u32[]{:S(2)}, u32[]{:S(2)}) collective-permute-start(bf16[2,128,256]{2,1,0:T(8,128)(2,1)S(1)} %get-tuple-element.40), channel_id=1, source_target_pairs={{0,66},{1,67},{4,70},{5,71},{8,74},{9,75},{12,78},{13,79},{64,2},{... | collective-permute-start | bytes 393224 | tf_op jit(solution)/shard_map/ppermute | solution.py:37
  9.9 5.3 %collective-permute-start.2 = (bf16[2,2,128,256]{3,2,1,0:T(8,128)(2,1)S(1)}, bf16[2,2,128,256]{3,2,1,0:T(8,128)(2,1)S(1)}, u32[]{:S(2)}, u32[]{:S(2)}) collective-permute-start(bf16[2,2,128,256]{3,2,1,0:T(8,128)(2,1)S(1)} %pad_maximum_fusion.3.refs_6_.refs_10_), channel_id=1, source_target_pairs={{0,4},{1,17},{4,0},{5,21},{8,12},{9,25},{12,8},{13,29},{64,68},{65... | collective-permute-start | bytes 786440 | tf_op jit(solution)/shard_map/ppermute | solution.py:37
  11.2 9.2 %collective-permute-start.5 = (bf16[2,2,128,256]{3,2,1,0:T(8,128)(2,1)S(1)}, bf16[2,2,128,256]{3,2,1,0:T(8,128)(2,1)S(1)}, u32[]{:S(2)}, u32[]{:S(2)}) collective-permute-start(bf16[2,2,128,256]{3,2,1,0:T(8,128)(2,1)S(1)} %pad_maximum_fusion.3.refs_6_.refs_10_), channel_id=1, source_target_pairs={{0,12},{1,49},{4,8},{5,53},{8,4},{9,57},{12,0},{13,61},{64,76},{65... | collective-permute-start | bytes 786440 | tf_op jit(solution)/shard_map/ppermute | solution.py:37
  13.1 7.3 %collective-permute-start.4 = (bf16[2,2,128,256]{3,2,1,0:T(8,128)(2,1)S(1)}, bf16[2,2,128,256]{3,2,1,0:T(8,128)(2,1)S(1)}, u32[]{:S(2)}, u32[]{:S(2)}) collective-permute-start(bf16[2,2,128,256]{3,2,1,0:T(8,128)(2,1)S(1)} %pad_maximum_fusion.3.refs_6_.refs_10_), channel_id=1, source_target_pairs={{0,8},{1,33},{4,12},{5,37},{8,0},{9,41},{12,4},{13,45},{64,72},{65... | collective-permute-start | bytes 786440 | tf_op jit(solution)/shard_map/ppermute | solution.py:37
  13.7 7.1 %copy-start = (bf16[128,1536]{1,0:T(8,128)(2,1)S(1)}, bf16[128,1536]{1,0:T(8,128)(2,1)}, u32[]{:S(2)}) copy-start(bf16[128,1536]{1,0:T(8,128)(2,1)} %queries_ref.1) | copy-start | bytes 1179652
  13.7 7.1 %copy-start.1 = (s32[16]{0:T(128)S(1)}, s32[16]{0:T(128)}, u32[]{:S(2)}) copy-start(s32[16]{0:T(128)} %refs_1_.5) | copy-start | bytes 196
  20.6 14.5 %collective-permute-start.6 = (bf16[4,2,128,256]{3,2,1,0:T(8,128)(2,1)S(1)}, bf16[4,2,128,256]{3,2,1,0:T(8,128)(2,1)S(1)}, u32[]{:S(2)}, u32[]{:S(2)}) collective-permute-start(bf16[4,2,128,256]{3,2,1,0:T(8,128)(2,1)S(1)} %pad_maximum_fusion), channel_id=1, source_target_pairs={{0,16},{1,5},{4,20},{5,1},{8,24},{9,13},{12,28},{13,9},{64,80},{65... | collective-permute-start | bytes 1572872 | tf_op jit(solution)/shard_map/ppermute | solution.py:37
  21.6 8.6 %collective-permute-start.3 = (bf16[1536,128]{1,0:T(8,128)(2,1)S(1)}, bf16[1536,128]{1,0:T(8,128)(2,1)S(1)}, u32[]{:S(2)}, u32[]{:S(2)}) collective-permute-start(bf16[1536,128]{1,0:T(8,128)(2,1)S(1)} %get-tuple-element.18.refs_4_), channel_id=1, source_target_pairs={{0,1},{1,0},{4,5},{5,4},{8,9},{9,8},{12,13},{13,12},{64,65},{65,64... | collective-permute-start | bytes 1179656 | tf_op jit(solution)/shard_map/ppermute | solution.py:37
  27.6 14.0 %collective-permute-start.7 = (bf16[4,2,128,256]{3,2,1,0:T(8,128)(2,1)S(1)}, bf16[4,2,128,256]{3,2,1,0:T(8,128)(2,1)S(1)}, u32[]{:S(2)}, u32[]{:S(2)}) collective-permute-start(bf16[4,2,128,256]{3,2,1,0:T(8,128)(2,1)S(1)} %pad_maximum_fusion.1), channel_id=1, source_target_pairs={{0,48},{1,13},{4,52},{5,9},{8,56},{9,5},{12,60},{13,1},{64,112},{6... | collective-permute-start | bytes 1572872 | tf_op jit(solution)/shard_map/ppermute | solution.py:37
  28.2 13.4 %collective-permute-start.8 = (bf16[4,2,128,256]{3,2,1,0:T(8,128)(2,1)S(1)}, bf16[4,2,128,256]{3,2,1,0:T(8,128)(2,1)S(1)}, u32[]{:S(2)}, u32[]{:S(2)}) collective-permute-start(bf16[4,2,128,256]{3,2,1,0:T(8,128)(2,1)S(1)} %pad_maximum_fusion.2), channel_id=1, source_target_pairs={{0,32},{1,9},{4,36},{5,13},{8,40},{9,1},{12,44},{13,5},{64,96},{65... | collective-permute-start | bytes 1572872 | tf_op jit(solution)/shard_map/ppermute | solution.py:37
  142.3 5.8 %collective-permute-start.9 = (bf16[128,1920]{1,0:T(8,128)(2,1)S(1)}, bf16[128,1920]{1,0:T(8,128)(2,1)S(1)}, u32[]{:S(2)}, u32[]{:S(2)}) collective-permute-start(bf16[128,1920]{1,0:T(8,128)(2,1)S(1)} %get-tuple-element.26), channel_id=1, source_target_pairs={{0,1},{1,0},{4,5},{5,4},{8,9},{9,8},{12,13},{13,12},{64,65},{65,64... | collective-permute-start | bytes 1474568 | tf_op jit(solution)/shard_map/ppermute | solution.py:37
